TPU v7x, 32 devices: a whole 2x2x4 slice. The times are simulated.
32 devices in a mesh: seq: 8 (over y, x, core), tensor: 4 (over z).
Axes of the slice: x: 2, y: 2, z: 4, core: 2. Of those that a mesh axis runs over, the one named last changes fastest.
Arguments:
- queries: bfloat16 [4096, 3072], P('seq', 'tensor'), may hold values from -180 to 180, as said below
- ref_keys: bfloat16 [128, 3072], P('seq', 'tensor'), may hold values from -6 to 6
- ref_values: bfloat16 [128, 3072], P('seq', 'tensor'), may hold values from -6 to 6
- grad_out: bfloat16 [4096, 3072], P('seq', 'tensor'), may hold values from -12 to 12
- key_weight: bfloat16 [3072, 3072], P(None, 'tensor'), may hold values from -0.109375 to 0.109375
- value_weight: bfloat16 [3072, 3072], P(None, 'tensor'), may hold values from -0.109375 to 0.109375
Outputs:
- grad_queries: bfloat16 [4096, 3072], P('seq', 'tensor')
- grad_ref_rows: bfloat16 [128, 3072], P('seq', 'tensor')
Inputs may be any that keep to these rules, and one draw needn't show every extreme that they name: `queries`: queries of order one, some rows larger.
All inputs are finite; a program needn't handle non-finite values.
Results may differ from a plain program's by a relative error of at most 0.015.
Values may be sent and summed in bfloat16 or wider, within the bound.
A program may use at most 128 MiB of HBM per device.

v0:
```python
import jax
import jax.numpy as jnp
from jax import lax
from jax.sharding import PartitionSpec as P

HD = 128


def head_terms(queries, keys_all, values_all, grad_out, head):
    scale = 1.0 / HD**0.5
    lo_col = head * HD
    query_h = queries[:, lo_col : lo_col + HD]
    key_h = keys_all[:, lo_col : lo_col + HD]
    value_h = values_all[:, lo_col : lo_col + HD]
    grad_h = grad_out[:, lo_col : lo_col + HD]
    scores = jnp.dot(query_h, key_h.T, preferred_element_type=jnp.float32) * scale
    probs = jax.nn.softmax(scores, axis=-1)
    probs_b = probs.astype(jnp.bfloat16)
    grad_probs = jnp.dot(grad_h, value_h.T, preferred_element_type=jnp.float32)
    delta = jnp.sum(probs * grad_probs, axis=-1, keepdims=True)
    grad_scores = (probs * (grad_probs - delta)).astype(jnp.bfloat16)
    grad_query = (jnp.dot(grad_scores, key_h, preferred_element_type=jnp.float32) * scale).astype(
        jnp.bfloat16
    )
    grad_key = jnp.dot(grad_scores.T, query_h, preferred_element_type=jnp.float32) * scale
    grad_value = jnp.dot(probs_b.T, grad_h, preferred_element_type=jnp.float32)
    return (grad_query, grad_key, grad_value)


def head_range(queries, keys_all, values_all, grad_out, first, count):
    query_list, key_list, value_list = ([], [], [])
    for head in range(first, first + count):
        grad_query, grad_key, grad_value = head_terms(queries, keys_all, values_all, grad_out, head)
        query_list.append(grad_query)
        key_list.append(grad_key)
        value_list.append(grad_value)
    return (query_list, jnp.concatenate(key_list, axis=1), jnp.concatenate(value_list, axis=1))


def project_exact(keys_own, values_own, key_weight, value_weight):
    key_cols = key_weight.astype(jnp.float32)
    value_cols = value_weight.astype(jnp.float32)
    rows = jnp.dot(
        keys_own, key_cols.T, precision=lax.Precision.HIGHEST, preferred_element_type=jnp.float32
    )
    return rows + jnp.dot(
        values_own,
        value_cols.T,
        precision=lax.Precision.HIGHEST,
        preferred_element_type=jnp.float32,
    )


def shards(queries, ref_keys, ref_values, grad_out, key_weight, value_weight):
    keys_all, values_all = (
        lax.all_gather(ref_keys, "seq", axis=0, tiled=True),
        lax.all_gather(ref_values, "seq", axis=0, tiled=True),
    )
    local_heads = queries.shape[1] // HD
    ranges = (0, local_heads)
    query_list = []
    first, count = ranges
    group_queries, key_terms, value_terms = head_range(
        queries, keys_all, values_all, grad_out, first, count
    )
    query_list = query_list + group_queries
    key_part = key_terms.astype(jnp.bfloat16)
    value_part = value_terms.astype(jnp.bfloat16)
    key_held, value_held = lax.optimization_barrier((key_part, value_part))
    key_wide = key_held.astype(jnp.float32)
    value_wide = value_held.astype(jnp.float32)
    keys_own = lax.psum_scatter(key_wide, "seq", scatter_dimension=0, tiled=True)
    values_own = lax.psum_scatter(value_wide, "seq", scatter_dimension=0, tiled=True)
    partial_value = project_exact(keys_own, values_own, key_weight, value_weight)
    grad_queries = jnp.concatenate(query_list, axis=1)
    grad_rows = lax.psum_scatter(
        partial_value.astype(jnp.bfloat16), "tensor", scatter_dimension=1, tiled=True
    )
    return (grad_queries, grad_rows)


def solution(mesh):
    placed = (
        P("seq", "tensor"),
        P("seq", "tensor"),
        P("seq", "tensor"),
        P("seq", "tensor"),
        P(None, "tensor"),
        P(None, "tensor"),
    )
    return jax.shard_map(
        shards,
        mesh=mesh,
        in_specs=placed,
        out_specs=(P("seq", "tensor"), P("seq", "tensor")),
        check_vma=False,
    )
```

profile of v0, /device:TPU:0, one launch (start us, length us, event | category | flops | bytes accessed | tf_op | source)
XLA Modules:
  0.0 145.6 jit_solution(7483940936679783050)
XLA Ops:
  7.2 11.0 %all_gather.6 = bf16[128,768]{1,0:T(8,128)(2,1)S(1)} all-gather(bf16[16,768]{1,0:T(8,128)(2,1)} %param.7), channel_id=1, replica_groups=mesh['seq'=8,'tensor'=4] {'seq'}, dimensions={0}, use_global_device_ids=true | all-gather | bytes 221184 | tf_op jit(solution)/shard_map/all_gather | solution.py:56
  18.3 1.1 fusion.103
  19.4 1.1 fusion.104
  20.5 1.1 fusion.105
  21.6 1.1 fusion.106
  22.7 1.1 fusion.107
  23.8 1.1 fusion.108
  24.9 9.1 %all_gather.7 = bf16[128,768]{1,0:T(8,128)(2,1)S(1)} all-gather(bf16[16,768]{1,0:T(8,128)(2,1)} %param.8), channel_id=1, replica_groups=mesh['seq'=8,'tensor'=4] {'seq'}, dimensions={0}, use_global_device_ids=true | all-gather | bytes 221184 | tf_op jit(solution)/shard_map/all_gather | solution.py:57
  34.1 1.1 fusion.30
  35.2 1.1 multiply_reduce_fusion.5
  36.3 0.1 fusion.34
  36.4 0.2 multiply_reduce_fusion.4
  36.6 0.2 fusion.29
  36.9 0.2 multiply_reduce_fusion.3
  37.1 0.2 fusion.28
  37.4 0.1 fusion.38
  37.4 0.2 multiply_reduce_fusion.2
  37.6 0.2 fusion.27
  37.9 0.2 multiply_reduce_fusion.1
  38.1 0.2 fusion.26
  38.5 0.2 multiply_reduce_fusion
  38.7 0.2 fusion.25
  38.9 0.1 multiply_convert_fusion.5
  39.0 0.2 fusion.14
  39.2 0.1 multiply_convert_fusion.4
  39.3 0.2 fusion.16
  39.6 0.1 multiply_convert_fusion.3
  39.6 0.2 fusion.18
  39.9 0.1 multiply_convert_fusion.2
  40.0 0.2 fusion.20
  40.2 0.1 multiply_convert_fusion.1
  40.3 0.2 fusion.22
  40.5 0.1 multiply_convert_fusion
  40.6 0.2 fusion.24
  40.9 0.9 copy.10
  41.8 0.9 copy.12
  42.8 0.2 fusion.2
  43.0 0.2 fusion.4
  43.2 0.2 fusion.6
  43.5 0.2 fusion.8
  43.7 0.2 fusion.10
  43.9 32.1 %reduce-scatter.10.cloned.1.call-done = f32[16,768]{1,0:T(8,128)} async-done(((f32[128,768]{1,0:T(8,128)}), f32[16,768]{1,0:T(8,128)}) %reduce-scatter.10.cloned.1.call-update) | async-done | bytes 49168
  76.1 6.1 %fusion.109 = f32[16,3072]{1,0:T(8,128)S(1)} fusion(f32[16,768]{1,0:T(8,128)} %reduce-scatter.10.cloned.1.call-done, bf16[3072,768]{1,0:T(8,128)(2,1)} %param.10), kind=kOutput, calls=%fused_computation.146 | convolution fusion | flops 452984832 | bytes 4964352 | tf_op jit(solution)/shard_map/dot_general | solution.py:43
  82.2 30.8 %reduce-scatter.12.cloned.1.call-done = f32[16,768]{1,0:T(8,128)} async-done(((f32[128,768]{1,0:T(8,128)}), f32[16,768]{1,0:T(8,128)}) %reduce-scatter.12.cloned.1.call-update) | async-done | bytes 49168
  113.0 6.8 %fusion = bf16[16,3072]{1,0:T(8,128)(2,1)} fusion(f32[16,3072]{1,0:T(8,128)S(1)} %fusion.109, f32[16,768]{1,0:T(8,128)} %reduce-scatter.12.cloned.1.call-done, bf16[3072,768]{1,0:T(8,128)(2,1)} %param.11), kind=kOutput, calls=%fused_computation.1 | convolution fusion | flops 453083136 | bytes 5062656 | tf_op jit(solution)/shard_map/dot_general | solution.py:46
  119.8 0.2 fusion.12
  120.0 1.2 copy.9
  121.2 17.9 %reduce-scatter.8.cloned.1.call-done = bf16[16,768]{1,0:T(8,128)(2,1)} async-done(((bf16[16,3072]{1,0:T(8,128)(2,1)}), bf16[16,768]{1,0:T(8,128)(2,1)}) %reduce-scatter.8.cloned.1.call-update) | async-done | bytes 24592 | tf_op jit(solution)/shard_map/reduce_scatter | solution.py:76
  (14 shorter events, 0.4 us)
Async XLA Ops:
  7.2 29.2 %copy-start.1 = (bf16[512,768]{1,0:T(8,128)(2,1)S(1)}, bf16[512,768]{1,0:T(8,128)(2,1)}, u32[]{:S(2)}) copy-start(bf16[512,768]{1,0:T(8,128)(2,1)} %param.9) | copy-start | bytes 2359300
  7.2 68.9 %reduce-scatter.10.cloned.1.call-start = ((), (), s32[]{:S(2)}) async-start(), calls=%async_computation.4 | async-start | bytes 442368
  37.3 1.6 %copy-start = (bf16[512,768]{1,0:T(8,128)(2,1)S(1)}, bf16[512,768]{1,0:T(8,128)(2,1)}, u32[]{:S(2)}) copy-start(bf16[512,768]{1,0:T(8,128)(2,1)} %param.6) | copy-start | bytes 2359300
  41.8 71.2 %reduce-scatter.12.cloned.1.call-start = ((), (), s32[]{:S(2)}) async-start(), calls=%async_computation.5 | async-start | bytes 442368
  42.7 96.3 %reduce-scatter.8.cloned.1.call-start = ((), (), s32[]{:S(2)}) async-start(), calls=%async_computation.3 | async-start | bytes 122880 | tf_op jit(solution)/shard_map/reduce_scatter | solution.py:76
Sparse Core Ops, SparseCore 0:
  41.9 34.1 reduce-scatter.9
  79.1 33.8 reduce-scatter.11
  119.9 19.0 reduce-scatter.7
where the time goes:
time: 146 us
  waiting for transfers between devices  80.9 us (55%)
  matrix products  26.8 us (18%)
  blocking collectives  20.1 us (14%)
  between operations  13.9 us (10%)
  local copies, waits for them, and re-layouts  2.95 us (2%)
    unnamed x5, waiting for transfers between devices  63 us
    reduce_scatter x1, waiting for transfers between devices, shards(): lax.psum_scatter(partial_value.astype(jnp.bfloat16), 'tensor', scatter_di...  17.9 us
    all_gather x1, blocking collectives, shards(): lax.all_gather(ref_keys, 'seq', axis=0, tiled=True)  11 us
    all_gather x1, blocking collectives, shards(): lax.all_gather(ref_values, 'seq', axis=0, tiled=True)  9.06 us
    dot_general x1, matrix products, project_exact(): jnp.dot(values_own, value_cols.T, precision=lax.Precision.HIGHEST, prefer...  6.75 us
    dot_general x6, matrix products, head_terms(): jnp.dot(query_h, key_h.T, preferred_element_type=jnp.float32) * scale  6.65 us
    dot_general x1, matrix products, project_exact(): jnp.dot(keys_own, key_cols.T, precision=lax.Precision.HIGHEST, preferred_...  6.11 us
    unnamed x7, local copies, waits for them, and re-layouts  2.95 us
  transfers between devices with their start and end apart: 3, of which 3 were waited for; matrix products, arithmetic and copies ran while one was open for 7% of the time, Pallas kernels for 0%

commit v1 on v0

v1 whole, which is shorter than its diff:
```python
import functools
import math

import jax
import jax.numpy as jnp
from jax import lax
from jax.experimental import pallas as pl
from jax.experimental.pallas import tpu as pltpu
from jax.sharding import PartitionSpec as P

HD = 128
SCALE = 1.0 / HD**0.5
EXP_SCALE = SCALE * math.log2(math.e)
MESH = pl.DeviceIdType.MESH
F32 = jnp.float32
BF16 = jnp.bfloat16


def each(lo, hi, body):
    if hi - lo <= 8:
        for i in range(lo, hi):
            body(i)
    else:

        def step(i, carry):
            body(i)
            return carry

        lax.fori_loop(lo, hi, step, 0)


def dot_nt(a, b):
    return lax.dot_general(a, b, (((1,), (1,)), ((), ())), preferred_element_type=F32)


def dot_tn(a, b):
    return lax.dot_general(a, b, (((0,), (0,)), ((), ())), preferred_element_type=F32)


def dot_nn(a, b):
    return jnp.dot(a, b, preferred_element_type=F32)


def attend(query, key, value, grad):
    scores = dot_nt(key, query)
    grad_probs = dot_nt(value, grad)
    top = jnp.max(scores, axis=0, keepdims=True)
    weights = jnp.exp2((scores - top) * EXP_SCALE)
    inverse = 1.0 / jnp.sum(weights, axis=0, keepdims=True)
    probs = weights * inverse
    delta = jnp.sum(probs * grad_probs, axis=0, keepdims=True)
    grad_scores = (probs * (grad_probs - delta)).astype(BF16)
    grad_query = (dot_tn(grad_scores, key) * SCALE).astype(BF16)
    grad_key = dot_nn(grad_scores, query) * SCALE
    grad_value = dot_nn(probs.astype(BF16), grad)
    return grad_query, grad_key, grad_value


def kernel(
    n,
    nt,
    groups,
    q_hbm,
    k_hbm,
    v_hbm,
    g_hbm,
    kw_hbm,
    vw_hbm,
    gq_hbm,
    rows_ref,
    q_buf,
    g_buf,
    gq_buf,
    w_buf,
    kv_buf,
    parts,
    got,
    sums,
    out_send,
    out_got,
    head_acc,
    in_sem,
    own_sem,
    w_sem,
    gq_sem,
    ag_send,
    ag_recv,
    aa_send,
    aa_recv,
    rs_send,
    rs_recv,
):
    me = lax.axis_index("seq")
    mt = lax.axis_index("tensor")
    tokens, width = q_hbm.shape
    own = k_hbm.shape[0]
    heads = width // HD
    per = heads // groups
    gw = per * HD
    out_cols = rows_ref.shape[1]
    my_rows = pl.ds(pl.multiple_of(me * own, own), own)

    own_copies = [
        pltpu.make_async_copy(k_hbm, kv_buf.at[0, my_rows], own_sem.at[0]),
        pltpu.make_async_copy(v_hbm, kv_buf.at[1, my_rows], own_sem.at[1]),
    ]
    for copy in own_copies:
        copy.start()
    in_copies = [
        pltpu.make_async_copy(q_hbm, q_buf, in_sem.at[0]),
        pltpu.make_async_copy(g_hbm, g_buf, in_sem.at[1]),
    ]
    for copy in in_copies:
        copy.start()

    barrier = pltpu.get_barrier_semaphore()

    def greet_seq(k):
        pl.semaphore_signal(
            barrier, inc=1, device_id={"seq": lax.rem(me + k, n)}, device_id_type=MESH
        )

    def greet_tensor(k):
        pl.semaphore_signal(
            barrier, inc=1, device_id={"tensor": lax.rem(mt + k, nt)}, device_id_type=MESH
        )

    each(1, nt, greet_tensor)
    each(1, n, greet_seq)
    for copy in own_copies:
        copy.wait()
    pl.semaphore_wait(barrier, n + nt - 2)

    for g in range(groups):
        cols = pl.ds(g * gw, gw)

        def send_rows(k, g=g, cols=cols):
            block = kv_buf.at[:, my_rows, cols]
            pltpu.make_async_remote_copy(
                src_ref=block,
                dst_ref=block,
                send_sem=ag_send,
                recv_sem=ag_recv.at[g],
                device_id={"seq": lax.rem(me + k, n)},
                device_id_type=MESH,
            ).start()

        each(1, n, send_rows)

    w_copies = [
        pltpu.make_async_copy(kw_hbm, w_buf.at[0], w_sem.at[0]),
        pltpu.make_async_copy(vw_hbm, w_buf.at[1], w_sem.at[1]),
    ]
    for copy in w_copies:
        copy.start()
    for copy in in_copies:
        copy.wait()

    ref_rows = n * own
    others = pl.ds(0, (n - 1) * own)
    small = ref_rows <= 256
    gq_copies = []
    for g in range(groups):
        cols = pl.ds(g * gw, gw)
        arrived = kv_buf.at[:, others, cols]
        pltpu.make_async_copy(arrived, arrived, ag_recv.at[g]).wait()

        def one_head(head):
            if isinstance(head, int):
                hc = pl.ds(head * HD, HD)
            else:
                hc = pl.ds(pl.multiple_of(head * HD, HD), HD)
            key = kv_buf[0, :, hc]
            value = kv_buf[1, :, hc]
            if small:
                grad_query, grad_key, grad_value = attend(q_buf[:, hc], key, value, g_buf[:, hc])
                gq_buf[:, hc] = grad_query
            else:
                head_acc[...] = jnp.zeros_like(head_acc)

                def chunk(c, carry):
                    tok = pl.ds(pl.multiple_of(c * HD, HD), HD)
                    gq, gk, gv = attend(q_buf[tok, hc], key, value, g_buf[tok, hc])
                    gq_buf[tok, hc] = gq
                    head_acc[0] += gk
                    head_acc[1] += gv
                    return carry

                lax.fori_loop(0, tokens // HD, chunk, 0)
                grad_key, grad_value = head_acc[0], head_acc[1]
            parts[0, :, hc] = grad_key.astype(BF16)
            parts[1, :, hc] = grad_value.astype(BF16)

        if small:
            for head in range(g * per, (g + 1) * per):
                one_head(head)
        else:
            lax.fori_loop(g * per, (g + 1) * per, lambda h, c: (one_head(h), c)[1], 0)

        def send_parts(k, g=g, cols=cols):
            to = lax.rem(me + k, n)
            pltpu.make_async_remote_copy(
                src_ref=parts.at[:, pl.ds(pl.multiple_of(to * own, own), own), cols],
                dst_ref=got.at[:, pl.ds((k - 1) * own, own), cols],
                send_sem=aa_send,
                recv_sem=aa_recv.at[g],
                device_id={"seq": to},
                device_id_type=MESH,
            ).start()

        each(1, n, send_parts)
        copy = pltpu.make_async_copy(gq_buf.at[:, cols], gq_hbm.at[:, cols], gq_sem.at[g])
        copy.start()
        gq_copies.append(copy)

    for copy in w_copies:
        copy.wait()
    rs_copies = []
    for g in range(groups):
        cols = pl.ds(g * gw, gw)
        arrived = got.at[:, :, cols]
        pltpu.make_async_copy(arrived, arrived, aa_recv.at[g]).wait()
        sides = []
        for side in range(2):
            total = parts[side, my_rows, cols].astype(F32)
            if n <= 8:
                for k in range(n - 1):
                    total += got[side, k * own : (k + 1) * own, cols].astype(F32)
            else:
                total = lax.fori_loop(
                    0,
                    n - 1,
                    lambda k, acc: acc
                    + got[side, pl.ds(pl.multiple_of(k * own, own), own), cols].astype(F32),
                    total,
                )
            high = total.astype(BF16)
            low = (total - high.astype(F32)).astype(BF16)
            sides.append(jnp.concatenate([high, low], axis=0))
        for j in range(1, nt + 1):
            to = lax.rem(mt + j, nt)
            wr = pl.ds(pl.multiple_of(to * out_cols, out_cols), out_cols)
            both = dot_nt(sides[0], w_buf[0, wr, cols]) + dot_nt(sides[1], w_buf[1, wr, cols])
            new = both[:own] + both[own:]
            if g:
                new = new + sums[j - 1]
            if g < groups - 1 or j == nt:
                sums[j - 1] = new
            else:
                out_send[j - 1] = new.astype(BF16)
                copy = pltpu.make_async_remote_copy(
                    src_ref=out_send.at[j - 1],
                    dst_ref=out_got.at[j - 1],
                    send_sem=rs_send.at[j - 1],
                    recv_sem=rs_recv.at[j - 1],
                    device_id={"tensor": to},
                    device_id_type=MESH,
                )
                copy.start()
                rs_copies.append(copy)

    sent = kv_buf.at[:, others]
    pltpu.make_async_copy(sent, sent, ag_send).wait()
    pltpu.make_async_copy(got, got, aa_send).wait()
    for copy in gq_copies:
        copy.wait()
    total = sums[nt - 1]
    for j, copy in enumerate(rs_copies):
        copy.wait_recv()
        total += out_got[j].astype(F32)
    rows_ref[...] = total.astype(BF16)
    for copy in rs_copies:
        copy.wait_send()


def solution(mesh):
    n, nt = mesh.shape["seq"], mesh.shape["tensor"]

    def shards(queries, ref_keys, ref_values, grad_out, key_weight, value_weight):
        tokens, width = queries.shape
        own = ref_keys.shape[0]
        features = key_weight.shape[0]
        heads = width // HD
        groups = 3 if heads % 3 == 0 else 1
        out_cols = features // nt
        any_spec = pl.BlockSpec(memory_space=pl.ANY)
        dma = pltpu.SemaphoreType.DMA
        return pl.pallas_call(
            functools.partial(kernel, n, nt, groups),
            out_shape=(
                jax.ShapeDtypeStruct((tokens, width), BF16),
                jax.ShapeDtypeStruct((own, out_cols), BF16),
            ),
            in_specs=[any_spec] * 6,
            out_specs=(any_spec, pl.BlockSpec(memory_space=pltpu.VMEM)),
            scratch_shapes=[
                pltpu.VMEM((tokens, width), BF16),
                pltpu.VMEM((tokens, width), BF16),
                pltpu.VMEM((tokens, width), BF16),
                pltpu.VMEM((2, features, width), BF16),
                pltpu.VMEM((2, n * own, width), BF16),
                pltpu.VMEM((2, n * own, width), BF16),
                pltpu.VMEM((2, (n - 1) * own, width), BF16),
                pltpu.VMEM((nt, own, out_cols), F32),
                pltpu.VMEM((nt - 1, own, out_cols), BF16),
                pltpu.VMEM((nt - 1, own, out_cols), BF16),
                pltpu.VMEM((2, n * own, HD), F32),
                dma((2,)),
                dma((2,)),
                dma((2,)),
                dma((groups,)),
                dma,
                dma((groups,)),
                dma,
                dma((groups,)),
                dma((nt - 1,)),
                dma((nt - 1,)),
            ],
            compiler_params=pltpu.CompilerParams(
                collective_id=0,
                has_side_effects=True,
                vmem_limit_bytes=48 * 1024 * 1024,
            ),
            cost_estimate=pl.CostEstimate(
                flops=1_000_000_000, bytes_accessed=12_000_000, transcendentals=400_000
            ),
        )(queries, ref_keys, ref_values, grad_out, key_weight, value_weight)

    placed = (
        P("seq", "tensor"),
        P("seq", "tensor"),
        P("seq", "tensor"),
        P("seq", "tensor"),
        P(None, "tensor"),
        P(None, "tensor"),
    )
    return jax.shard_map(
        shards,
        mesh=mesh,
        in_specs=placed,
        out_specs=(P("seq", "tensor"), P("seq", "tensor")),
        check_vma=False,
    )
```

time: 146 us -> 27.8 us (0.19)
  waiting for transfers between devices: 80.9 us -> 0 us
  matrix products: 26.8 us -> 0 us
  Pallas kernels: 0 us -> 21.6 us
  blocking collectives: 20.1 us -> 0 us
  between operations: 13.9 us -> 0.65 us
  local copies, waits for them, and re-layouts: 2.95 us -> 5.22 us
    unnamed x5 -> x0, waiting for transfers between devices: 63 us -> none
    dot_general x32 -> x0, matrix products: 26.8 us -> none  [the longest x1 6.75 us: project_exact(): jnp.dot(values_own, value_cols.T, precision=lax.Precision.HIGHEST, prefer...]
    pallas_call x0 -> x1, Pallas kernels: none -> 21.6 us  [shards(): pl.pallas_call(functools.partial(kernel, n, nt, groups), out_shape=(jax.S...]
    all_gather x2 -> x0, blocking collectives: 20.1 us -> none  [the longest x1 11 us: shards(): lax.all_gather(ref_keys, 'seq', axis=0, tiled=True)]
    reduce_scatter x1 -> x0, waiting for transfers between devices: 17.9 us -> none  [shards(): lax.psum_scatter(partial_value.astype(jnp.bfloat16), 'tensor', scatter_di...]
    unnamed x7 -> x10, local copies, waits for them, and re-layouts: 2.95 us -> 5.22 us
  transfers between devices with their start and end apart: 3 -> 0, of which waited for: 3 -> 0; matrix products, arithmetic and copies ran while one was open for 7% -> 0% of each run, Pallas kernels for 0% -> 0%
where the time goes in v1:
time: 27.8 us; the launch traced here: 27.5 us
  Pallas kernels  21.6 us (78%)
  local copies, waits for them, and re-layouts  5.22 us (19%)
  between operations  0.65 us (2%)
    pallas_call x1, Pallas kernels, shards(): pl.pallas_call(functools.partial(kernel, n, nt, groups), out_shape=(jax.S...  21.6 us
    unnamed x10, local copies, waits for them, and re-layouts  5.22 us

profile of v1, /device:TPU:0, one launch (start us, length us, event | category | flops | bytes accessed | tf_op | source)
XLA Modules:
  0.0 27.5 jit_solution(15073764391125775905)
XLA Ops:
  0.6 0.0 copy-start
  0.6 1.1 %copy-done = bf16[512,768]{1,0:T(8,128)(2,1)S(1)} copy-done((bf16[512,768]{1,0:T(8,128)(2,1)S(1)}, bf16[512,768]{1,0:T(8,128)(2,1)}, u32[]{:S(2)}) %copy-start) | copy-done | bytes 786456
  1.8 0.0 copy-start.1
  1.8 1.1 %copy-done.1 = bf16[512,768]{1,0:T(8,128)(2,1)S(1)} copy-done((bf16[512,768]{1,0:T(8,128)(2,1)S(1)}, bf16[512,768]{1,0:T(8,128)(2,1)}, u32[]{:S(2)}) %copy-start.1) | copy-done | bytes 786456
  2.9 0.0 copy-start.2
  2.9 0.7 %copy-done.2 = bf16[16,768]{1,0:T(8,128)(2,1)S(1)} copy-done((bf16[16,768]{1,0:T(8,128)(2,1)S(1)}, bf16[16,768]{1,0:T(8,128)(2,1)}, u32[]{:S(2)}) %copy-start.2) | copy-done | bytes 24600
  3.6 0.0 copy-start.3
  3.6 0.7 %copy-done.3 = bf16[16,768]{1,0:T(8,128)(2,1)S(1)} copy-done((bf16[16,768]{1,0:T(8,128)(2,1)S(1)}, bf16[16,768]{1,0:T(8,128)(2,1)}, u32[]{:S(2)}) %copy-start.3) | copy-done | bytes 24600
  4.4 21.6 %shard_map.77 = (bf16[512,768]{1,0:T(8,128)(2,1)S(1)}, bf16[16,768]{1,0:T(8,128)(2,1)S(1)}) custom-call(bf16[512,768]{1,0:T(8,128)(2,1)S(1)} %copy-done, bf16[16,768]{1,0:T(8,128)(2,1)S(1)} %copy-done.2, bf16[16,768]{1,0:T(8,128)(2,1)S(1)} %copy-done.3, bf16[512,768]{1,0:T(8,128)(2,1)S(1)} %copy-done.1, bf16[3072,768]{1,0:T(8,128)(2,1)} %kw_hbm.1, ...), custom_call_target="tpu_custom_call" | custom-call | flops 1000000000 | bytes 12000000 | tf_op jit(solution)/shard_map/pallas_call | solution.py:288
  26.0 0.9 %copy.10 = bf16[512,768]{1,0:T(8,128)(2,1)} copy(bf16[512,768]{1,0:T(8,128)(2,1)S(1)} %get-tuple-element.4) | data formatting | bytes 1572864
  26.9 0.6 %copy.11 = bf16[16,768]{1,0:T(8,128)(2,1)} copy(bf16[16,768]{1,0:T(8,128)(2,1)S(1)} %get-tuple-element.5) | data formatting | bytes 49152
Async XLA Ops:
  0.6 1.1 %copy-start = (bf16[512,768]{1,0:T(8,128)(2,1)S(1)}, bf16[512,768]{1,0:T(8,128)(2,1)}, u32[]{:S(2)}) copy-start(bf16[512,768]{1,0:T(8,128)(2,1)} %q_hbm.1) | copy-start | bytes 2359300
  1.8 1.1 %copy-start.1 = (bf16[512,768]{1,0:T(8,128)(2,1)S(1)}, bf16[512,768]{1,0:T(8,128)(2,1)}, u32[]{:S(2)}) copy-start(bf16[512,768]{1,0:T(8,128)(2,1)} %g_hbm.1) | copy-start | bytes 2359300
  2.9 0.7 %copy-start.2 = (bf16[16,768]{1,0:T(8,128)(2,1)S(1)}, bf16[16,768]{1,0:T(8,128)(2,1)}, u32[]{:S(2)}) copy-start(bf16[16,768]{1,0:T(8,128)(2,1)} %k_hbm.1) | copy-start | bytes 73732
  3.6 0.7 %copy-start.3 = (bf16[16,768]{1,0:T(8,128)(2,1)S(1)}, bf16[16,768]{1,0:T(8,128)(2,1)}, u32[]{:S(2)}) copy-start(bf16[16,768]{1,0:T(8,128)(2,1)} %v_hbm.1) | copy-start | bytes 73732

commit v2 on v1

--- a/solution.py
+++ b/solution.py
@@ -9,6 +9,8 @@
 from jax.sharding import PartitionSpec as P
 
 HD = 128
+CHUNK = 256
+VMEM_LIMIT = 60 * 1024 * 1024
 SCALE = 1.0 / HD**0.5
 EXP_SCALE = SCALE * math.log2(math.e)
 MESH = pl.DeviceIdType.MESH
@@ -50,10 +52,9 @@
     probs = weights * inverse
     delta = jnp.sum(probs * grad_probs, axis=0, keepdims=True)
     grad_scores = (probs * (grad_probs - delta)).astype(BF16)
-    grad_query = (dot_tn(grad_scores, key) * SCALE).astype(BF16)
-    grad_key = dot_nn(grad_scores, query) * SCALE
+    grad_key = dot_nn(grad_scores, query)
     grad_value = dot_nn(probs.astype(BF16), grad)
-    return grad_query, grad_key, grad_value
+    return grad_scores, grad_key, grad_value
 
 
 def kernel(
@@ -71,6 +72,7 @@
     q_buf,
     g_buf,
     gq_buf,
+    ds_buf,
     w_buf,
     kv_buf,
     parts,
@@ -159,7 +161,6 @@
     ref_rows = n * own
     others = pl.ds(0, (n - 1) * own)
     small = ref_rows <= 256
-    gq_copies = []
     for g in range(groups):
         cols = pl.ds(g * gw, gw)
         arrived = kv_buf.at[:, others, cols]
@@ -173,22 +174,27 @@
             key = kv_buf[0, :, hc]
             value = kv_buf[1, :, hc]
             if small:
-                grad_query, grad_key, grad_value = attend(q_buf[:, hc], key, value, g_buf[:, hc])
-                gq_buf[:, hc] = grad_query
+                grad_key = grad_value = None
+                for lo in range(0, tokens, CHUNK):
+                    tok = slice(lo, min(lo + CHUNK, tokens))
+                    ds, gk, gv = attend(q_buf[tok, hc], key, value, g_buf[tok, hc])
+                    ds_buf[head, :, tok] = ds
+                    grad_key = gk if grad_key is None else grad_key + gk
+                    grad_value = gv if grad_value is None else grad_value + gv
             else:
                 head_acc[...] = jnp.zeros_like(head_acc)
 
                 def chunk(c, carry):
                     tok = pl.ds(pl.multiple_of(c * HD, HD), HD)
-                    gq, gk, gv = attend(q_buf[tok, hc], key, value, g_buf[tok, hc])
-                    gq_buf[tok, hc] = gq
+                    ds, gk, gv = attend(q_buf[tok, hc], key, value, g_buf[tok, hc])
+                    ds_buf[head, :, tok] = ds
                     head_acc[0] += gk
                     head_acc[1] += gv
                     return carry
 
                 lax.fori_loop(0, tokens // HD, chunk, 0)
                 grad_key, grad_value = head_acc[0], head_acc[1]
-            parts[0, :, hc] = grad_key.astype(BF16)
+            parts[0, :, hc] = (grad_key * SCALE).astype(BF16)
             parts[1, :, hc] = grad_value.astype(BF16)
 
         if small:
@@ -209,6 +215,23 @@
             ).start()
 
         each(1, n, send_parts)
+
+    gq_copies = []
+
+    def query_grads(g):
+        def one_head(head):
+            if isinstance(head, int):
+                hc = pl.ds(head * HD, HD)
+            else:
+                hc = pl.ds(pl.multiple_of(head * HD, HD), HD)
+            gq_buf[:, hc] = (dot_tn(ds_buf[head], kv_buf[0, :, hc]) * SCALE).astype(BF16)
+
+        if small:
+            for head in range(g * per, (g + 1) * per):
+                one_head(head)
+        else:
+            lax.fori_loop(g * per, (g + 1) * per, lambda h, c: (one_head(h), c)[1], 0)
+        cols = pl.ds(g * gw, gw)
         copy = pltpu.make_async_copy(gq_buf.at[:, cols], gq_hbm.at[:, cols], gq_sem.at[g])
         copy.start()
         gq_copies.append(copy)
@@ -217,6 +240,8 @@
         copy.wait()
     rs_copies = []
     for g in range(groups):
+        if g < groups - 1:
+            query_grads(g)
         cols = pl.ds(g * gw, gw)
         arrived = got.at[:, :, cols]
         pltpu.make_async_copy(arrived, arrived, aa_recv.at[g]).wait()
@@ -259,10 +284,11 @@
                 copy.start()
                 rs_copies.append(copy)
 
+    query_grads(groups - 1)
     sent = kv_buf.at[:, others]
     pltpu.make_async_copy(sent, sent, ag_send).wait()
     pltpu.make_async_copy(got, got, aa_send).wait()
-    for copy in gq_copies:
+    for copy in gq_copies[:-1]:
         copy.wait()
     total = sums[nt - 1]
     for j, copy in enumerate(rs_copies):
@@ -271,6 +297,18 @@
     rows_ref[...] = total.astype(BF16)
     for copy in rs_copies:
         copy.wait_send()
+    gq_copies[-1].wait()
+
+
+def deliver(gq_ref, rows_ref, gq_out, rows_out, sem):
+    copies = [
+        pltpu.make_async_copy(gq_ref, gq_out, sem.at[0]),
+        pltpu.make_async_copy(rows_ref, rows_out, sem.at[1]),
+    ]
+    for copy in copies:
+        copy.start()
+    for copy in copies:
+        copy.wait()
 
 
 def solution(mesh):
@@ -283,20 +321,22 @@
         heads = width // HD
         groups = 3 if heads % 3 == 0 else 1
         out_cols = features // nt
-        any_spec = pl.BlockSpec(memory_space=pl.ANY)
+        hbm_spec = pl.BlockSpec(memory_space=pltpu.HBM)
+        vmem_spec = pl.BlockSpec(memory_space=pltpu.VMEM)
         dma = pltpu.SemaphoreType.DMA
-        return pl.pallas_call(
+        held = pl.pallas_call(
             functools.partial(kernel, n, nt, groups),
             out_shape=(
                 jax.ShapeDtypeStruct((tokens, width), BF16),
                 jax.ShapeDtypeStruct((own, out_cols), BF16),
             ),
-            in_specs=[any_spec] * 6,
-            out_specs=(any_spec, pl.BlockSpec(memory_space=pltpu.VMEM)),
+            in_specs=[hbm_spec] * 6,
+            out_specs=(hbm_spec, vmem_spec),
             scratch_shapes=[
                 pltpu.VMEM((tokens, width), BF16),
                 pltpu.VMEM((tokens, width), BF16),
                 pltpu.VMEM((tokens, width), BF16),
+                pltpu.VMEM((heads, n * own, tokens), BF16),
                 pltpu.VMEM((2, features, width), BF16),
                 pltpu.VMEM((2, n * own, width), BF16),
                 pltpu.VMEM((2, n * own, width), BF16),
@@ -319,12 +359,23 @@
             compiler_params=pltpu.CompilerParams(
                 collective_id=0,
                 has_side_effects=True,
-                vmem_limit_bytes=48 * 1024 * 1024,
+                vmem_limit_bytes=VMEM_LIMIT,
             ),
             cost_estimate=pl.CostEstimate(
                 flops=1_000_000_000, bytes_accessed=12_000_000, transcendentals=400_000
             ),
         )(queries, ref_keys, ref_values, grad_out, key_weight, value_weight)
+        return pl.pallas_call(
+            deliver,
+            out_shape=(
+                jax.ShapeDtypeStruct((tokens, width), BF16),
+                jax.ShapeDtypeStruct((own, out_cols), BF16),
+            ),
+            in_specs=[hbm_spec] * 2,
+            out_specs=(hbm_spec, hbm_spec),
+            scratch_shapes=[dma((2,))],
+            compiler_params=pltpu.CompilerParams(vmem_limit_bytes=VMEM_LIMIT),
+        )(*held)
 
     placed = (
         P("seq", "tensor"),

time: 27.8 us -> 48.5 us (1.74)
  Pallas kernels: 21.6 us -> 47.7 us
  local copies, waits for them, and re-layouts: 5.22 us -> 0 us
    pallas_call x0 -> x1, Pallas kernels: none -> 25.7 us  [shards(): pl.pallas_call(deliver, out_shape=(jax.ShapeDtypeStruct((tokens, width),...]
    unnamed x10 -> x0, local copies, waits for them, and re-layouts: 5.22 us -> none
where the time goes in v2:
time: 48.5 us; the launch traced here: 48.3 us
  Pallas kernels  47.7 us (98%)
  between operations  0.64 us (1%)
    pallas_call x1, Pallas kernels, shards(): pl.pallas_call(deliver, out_shape=(jax.ShapeDtypeStruct((tokens, width),...  25.7 us
    pallas_call x1, Pallas kernels, shards(): pl.pallas_call(functools.partial(kernel, n, nt, groups), out_shape=(jax.S...  22 us

profile of v2, /device:TPU:0, one launch (start us, length us, event | category | flops | bytes accessed | tf_op | source)
XLA Modules:
  0.0 48.3 jit_solution(3659449576296580333)
XLA Ops:
  0.6 22.0 %shard_map.77 = (bf16[512,768]{1,0:T(8,128)(2,1)}, bf16[16,768]{1,0:T(8,128)(2,1)}) custom-call(bf16[512,768]{1,0:T(8,128)(2,1)} %q_hbm.1, bf16[16,768]{1,0:T(8,128)(2,1)} %k_hbm.1, bf16[16,768]{1,0:T(8,128)(2,1)} %v_hbm.1, bf16[512,768]{1,0:T(8,128)(2,1)} %g_hbm.1, bf16[3072,768]{1,0:T(8,128)(2,1)} %kw_hbm.1, bf16[3072,768]{1,0:T(8,128)(2,1)} %vw_hbm.1), custom_call_target="tpu_custom_call" | custom-call | flops 1000000000 | bytes 12000000 | tf_op jit(solution)/shard_map/pallas_call | solution.py:327
  22.6 25.7 %shard_map.78 = (bf16[512,768]{1,0:T(8,128)(2,1)}, bf16[16,768]{1,0:T(8,128)(2,1)}) custom-call(bf16[512,768]{1,0:T(8,128)(2,1)} %get-tuple-element.4.gq_ref, bf16[16,768]{1,0:T(8,128)(2,1)} %get-tuple-element.5.rows_ref), custom_call_target="tpu_custom_call" | custom-call | tf_op jit(solution)/shard_map/pallas_call | solution.py:368

commit v3 on v2

--- a/solution.py
+++ b/solution.py
@@ -10,7 +10,8 @@
 
 HD = 128
 CHUNK = 256
-VMEM_LIMIT = 60 * 1024 * 1024
+SPLIT = 4
+VMEM_LIMIT = 48 * 1024 * 1024
 SCALE = 1.0 / HD**0.5
 EXP_SCALE = SCALE * math.log2(math.e)
 MESH = pl.DeviceIdType.MESH
@@ -67,11 +68,10 @@
     g_hbm,
     kw_hbm,
     vw_hbm,
-    gq_hbm,
+    gq_buf,
     rows_ref,
     q_buf,
     g_buf,
-    gq_buf,
     ds_buf,
     w_buf,
     kv_buf,
@@ -84,7 +84,6 @@
     in_sem,
     own_sem,
     w_sem,
-    gq_sem,
     ag_send,
     ag_recv,
     aa_send,
@@ -216,8 +215,6 @@
 
         each(1, n, send_parts)
 
-    gq_copies = []
-
     def query_grads(g):
         def one_head(head):
             if isinstance(head, int):
@@ -231,10 +228,6 @@
                 one_head(head)
         else:
             lax.fori_loop(g * per, (g + 1) * per, lambda h, c: (one_head(h), c)[1], 0)
-        cols = pl.ds(g * gw, gw)
-        copy = pltpu.make_async_copy(gq_buf.at[:, cols], gq_hbm.at[:, cols], gq_sem.at[g])
-        copy.start()
-        gq_copies.append(copy)
 
     for copy in w_copies:
         copy.wait()
@@ -288,8 +281,6 @@
     sent = kv_buf.at[:, others]
     pltpu.make_async_copy(sent, sent, ag_send).wait()
     pltpu.make_async_copy(got, got, aa_send).wait()
-    for copy in gq_copies[:-1]:
-        copy.wait()
     total = sums[nt - 1]
     for j, copy in enumerate(rs_copies):
         copy.wait_recv()
@@ -297,14 +288,14 @@
     rows_ref[...] = total.astype(BF16)
     for copy in rs_copies:
         copy.wait_send()
-    gq_copies[-1].wait()
 
 
 def deliver(gq_ref, rows_ref, gq_out, rows_out, sem):
-    copies = [
-        pltpu.make_async_copy(gq_ref, gq_out, sem.at[0]),
-        pltpu.make_async_copy(rows_ref, rows_out, sem.at[1]),
-    ]
+    part = gq_ref.shape[0] // SPLIT
+    copies = [pltpu.make_async_copy(rows_ref, rows_out, sem.at[SPLIT])]
+    for i in range(SPLIT):
+        rows = pl.ds(i * part, part)
+        copies.append(pltpu.make_async_copy(gq_ref.at[rows], gq_out.at[rows], sem.at[i]))
     for copy in copies:
         copy.start()
     for copy in copies:
@@ -327,13 +318,12 @@
         held = pl.pallas_call(
             functools.partial(kernel, n, nt, groups),
             out_shape=(
-                jax.ShapeDtypeStruct((tokens, width), BF16),
-                jax.ShapeDtypeStruct((own, out_cols), BF16),
+                pltpu.VMEM((tokens, width), BF16),
+                pltpu.VMEM((own, out_cols), BF16),
             ),
             in_specs=[hbm_spec] * 6,
-            out_specs=(hbm_spec, vmem_spec),
+            out_specs=(vmem_spec, vmem_spec),
             scratch_shapes=[
-                pltpu.VMEM((tokens, width), BF16),
                 pltpu.VMEM((tokens, width), BF16),
                 pltpu.VMEM((tokens, width), BF16),
                 pltpu.VMEM((heads, n * own, tokens), BF16),
@@ -348,7 +338,6 @@
                 dma((2,)),
                 dma((2,)),
                 dma((2,)),
-                dma((groups,)),
                 dma,
                 dma((groups,)),
                 dma,
@@ -364,17 +353,21 @@
             cost_estimate=pl.CostEstimate(
                 flops=1_000_000_000, bytes_accessed=12_000_000, transcendentals=400_000
             ),
-        )(queries, ref_keys, ref_values, grad_out, key_weight, value_weight)
+        )(
+            *(
+                pltpu.with_memory_space_constraint(x, pltpu.HBM)
+                for x in (queries, ref_keys, ref_values, grad_out, key_weight, value_weight)
+            )
+        )
         return pl.pallas_call(
             deliver,
             out_shape=(
                 jax.ShapeDtypeStruct((tokens, width), BF16),
                 jax.ShapeDtypeStruct((own, out_cols), BF16),
             ),
-            in_specs=[hbm_spec] * 2,
+            in_specs=[vmem_spec] * 2,
             out_specs=(hbm_spec, hbm_spec),
-            scratch_shapes=[dma((2,))],
-            compiler_params=pltpu.CompilerParams(vmem_limit_bytes=VMEM_LIMIT),
+            scratch_shapes=[dma((SPLIT + 1,))],
         )(*held)
 
     placed = (

time: 48.5 us -> 25.7 us (0.53)
  Pallas kernels: 47.7 us -> 23.4 us
  local copies, waits for them, and re-layouts: 0 us -> 1.5 us
    pallas_call x1, Pallas kernels: 25.7 us -> 2.06 us  [shards(): pl.pallas_call(deliver, out_shape=(jax.ShapeDtypeStruct((tokens, width),...]
    unnamed x0 -> x4, local copies, waits for them, and re-layouts: none -> 1.5 us
    pallas_call x1, Pallas kernels: 22 us -> 21.4 us  [shards(): pl.pallas_call(functools.partial(kernel, n, nt, groups), out_shape=(pltpu...]
where the time goes in v3:
time: 25.7 us; the launch traced here: 25.6 us
  Pallas kernels  23.4 us (91%)
  local copies, waits for them, and re-layouts  1.5 us (6%)
  between operations  0.65 us (3%)
    pallas_call x1, Pallas kernels, shards(): pl.pallas_call(functools.partial(kernel, n, nt, groups), out_shape=(pltpu...  21.4 us
    pallas_call x1, Pallas kernels, shards(): pl.pallas_call(deliver, out_shape=(jax.ShapeDtypeStruct((tokens, width),...  2.06 us
    unnamed x4, local copies, waits for them, and re-layouts  1.5 us

profile of v3, /device:TPU:0, one launch (start us, length us, event | category | flops | bytes accessed | tf_op | source)
XLA Modules:
  0.0 25.6 jit_solution(16635962574616969591)
XLA Ops:
  0.6 21.4 %shard_map.77 = (bf16[512,768]{1,0:T(8,128)(2,1)S(1)}, bf16[16,768]{1,0:T(8,128)(2,1)S(1)}) custom-call(bf16[512,768]{1,0:T(8,128)(2,1)} %q_hbm.1, bf16[16,768]{1,0:T(8,128)(2,1)} %k_hbm.1, bf16[16,768]{1,0:T(8,128)(2,1)} %v_hbm.1, bf16[512,768]{1,0:T(8,128)(2,1)} %g_hbm.1, bf16[3072,768]{1,0:T(8,128)(2,1)} %kw_hbm.1, bf16[3072,768]{1,0:T(8,128)(2,1)} %vw_hbm.1), custom_call_target="tpu_custom_call" | custom-call | flops 1000000000 | bytes 12000000 | tf_op jit(solution)/shard_map/pallas_call | solution.py:318
  22.0 0.0 copy-start
  22.0 0.9 %copy-done = bf16[512,768]{1,0:T(8,128)(2,1)} copy-done((bf16[512,768]{1,0:T(8,128)(2,1)}, bf16[512,768]{1,0:T(8,128)(2,1)S(1)}, u32[]{:S(2)}) %copy-start) | copy-done | bytes 786456
  22.9 0.0 copy-start.1
  22.9 0.6 %copy-done.1 = bf16[16,768]{1,0:T(8,128)(2,1)} copy-done((bf16[16,768]{1,0:T(8,128)(2,1)}, bf16[16,768]{1,0:T(8,128)(2,1)S(1)}, u32[]{:S(2)}) %copy-start.1) | copy-done | bytes 24600
  23.5 2.1 %shard_map.78 = (bf16[512,768]{1,0:T(8,128)(2,1)}, bf16[16,768]{1,0:T(8,128)(2,1)}) custom-call(bf16[512,768]{1,0:T(8,128)(2,1)} %copy-done, bf16[16,768]{1,0:T(8,128)(2,1)} %copy-done.1), custom_call_target="tpu_custom_call" | custom-call | tf_op jit(solution)/shard_map/pallas_call | solution.py:362
Async XLA Ops:
  22.0 0.9 %copy-start = (bf16[512,768]{1,0:T(8,128)(2,1)}, bf16[512,768]{1,0:T(8,128)(2,1)S(1)}, u32[]{:S(2)}) copy-start(bf16[512,768]{1,0:T(8,128)(2,1)S(1)} %get-tuple-element.4.gq_ref) | copy-start | bytes 2359300
  22.9 0.6 %copy-start.1 = (bf16[16,768]{1,0:T(8,128)(2,1)}, bf16[16,768]{1,0:T(8,128)(2,1)S(1)}, u32[]{:S(2)}) copy-start(bf16[16,768]{1,0:T(8,128)(2,1)S(1)} %get-tuple-element.5.rows_ref) | copy-start | bytes 73732

commit v4 on v3

--- a/solution.py
+++ b/solution.py
@@ -62,6 +62,7 @@
     n,
     nt,
     groups,
+    cuts,
     q_hbm,
     k_hbm,
     v_hbm,
@@ -101,6 +102,20 @@
     out_cols = rows_ref.shape[1]
     my_rows = pl.ds(pl.multiple_of(me * own, own), own)
 
+    barrier = pltpu.get_barrier_semaphore()
+
+    def greet_seq(k):
+        pl.semaphore_signal(
+            barrier, inc=1, device_id={"seq": lax.rem(me + k, n)}, device_id_type=MESH
+        )
+
+    def greet_tensor(k):
+        pl.semaphore_signal(
+            barrier, inc=1, device_id={"tensor": lax.rem(mt + k, nt)}, device_id_type=MESH
+        )
+
+    each(1, n, greet_seq)
+    each(1, nt, greet_tensor)
     own_copies = [
         pltpu.make_async_copy(k_hbm, kv_buf.at[0, my_rows], own_sem.at[0]),
         pltpu.make_async_copy(v_hbm, kv_buf.at[1, my_rows], own_sem.at[1]),
@@ -114,34 +129,20 @@
     for copy in in_copies:
         copy.start()
 
-    barrier = pltpu.get_barrier_semaphore()
-
-    def greet_seq(k):
-        pl.semaphore_signal(
-            barrier, inc=1, device_id={"seq": lax.rem(me + k, n)}, device_id_type=MESH
-        )
-
-    def greet_tensor(k):
-        pl.semaphore_signal(
-            barrier, inc=1, device_id={"tensor": lax.rem(mt + k, nt)}, device_id_type=MESH
-        )
-
-    each(1, nt, greet_tensor)
-    each(1, n, greet_seq)
     for copy in own_copies:
         copy.wait()
     pl.semaphore_wait(barrier, n + nt - 2)
 
-    for g in range(groups):
-        cols = pl.ds(g * gw, gw)
-
-        def send_rows(k, g=g, cols=cols):
+    for c, (first, count) in enumerate(cuts):
+        cols = pl.ds(first * HD, count * HD)
+
+        def send_rows(k, c=c, cols=cols):
             block = kv_buf.at[:, my_rows, cols]
             pltpu.make_async_remote_copy(
                 src_ref=block,
                 dst_ref=block,
                 send_sem=ag_send,
-                recv_sem=ag_recv.at[g],
+                recv_sem=ag_recv.at[c],
                 device_id={"seq": lax.rem(me + k, n)},
                 device_id_type=MESH,
             ).start()
@@ -160,10 +161,15 @@
     ref_rows = n * own
     others = pl.ds(0, (n - 1) * own)
     small = ref_rows <= 256
+
+    def await_rows(c):
+        first, count = cuts[c]
+        arrived = kv_buf.at[:, others, pl.ds(first * HD, count * HD)]
+        pltpu.make_async_copy(arrived, arrived, ag_recv.at[c]).wait()
+
+    starts = [first for first, _ in cuts]
     for g in range(groups):
         cols = pl.ds(g * gw, gw)
-        arrived = kv_buf.at[:, others, cols]
-        pltpu.make_async_copy(arrived, arrived, ag_recv.at[g]).wait()
 
         def one_head(head):
             if isinstance(head, int):
@@ -198,8 +204,13 @@
 
         if small:
             for head in range(g * per, (g + 1) * per):
+                if head in starts:
+                    await_rows(starts.index(head))
                 one_head(head)
         else:
+            for head in range(g * per, (g + 1) * per):
+                if head in starts:
+                    await_rows(starts.index(head))
             lax.fori_loop(g * per, (g + 1) * per, lambda h, c: (one_head(h), c)[1], 0)
 
         def send_parts(k, g=g, cols=cols):
@@ -233,7 +244,7 @@
         copy.wait()
     rs_copies = []
     for g in range(groups):
-        if g < groups - 1:
+        if g == 0:
             query_grads(g)
         cols = pl.ds(g * gw, gw)
         arrived = got.at[:, :, cols]
@@ -277,7 +288,8 @@
                 copy.start()
                 rs_copies.append(copy)
 
-    query_grads(groups - 1)
+    for g in range(1, groups):
+        query_grads(g)
     sent = kv_buf.at[:, others]
     pltpu.make_async_copy(sent, sent, ag_send).wait()
     pltpu.make_async_copy(got, got, aa_send).wait()
@@ -290,6 +302,16 @@
         copy.wait_send()
 
 
+def gather_cuts(heads):
+    cuts = []
+    at = 0
+    while at < heads:
+        count = min(1 if at < 2 else 2, heads - at)
+        cuts.append((at, count))
+        at += count
+    return cuts
+
+
 def deliver(gq_ref, rows_ref, gq_out, rows_out, sem):
     part = gq_ref.shape[0] // SPLIT
     copies = [pltpu.make_async_copy(rows_ref, rows_out, sem.at[SPLIT])]
@@ -311,12 +333,13 @@
         features = key_weight.shape[0]
         heads = width // HD
         groups = 3 if heads % 3 == 0 else 1
+        cuts = gather_cuts(heads)
         out_cols = features // nt
         hbm_spec = pl.BlockSpec(memory_space=pltpu.HBM)
         vmem_spec = pl.BlockSpec(memory_space=pltpu.VMEM)
         dma = pltpu.SemaphoreType.DMA
         held = pl.pallas_call(
-            functools.partial(kernel, n, nt, groups),
+            functools.partial(kernel, n, nt, groups, cuts),
             out_shape=(
                 pltpu.VMEM((tokens, width), BF16),
                 pltpu.VMEM((own, out_cols), BF16),
@@ -339,7 +362,7 @@
                 dma((2,)),
                 dma((2,)),
                 dma,
-                dma((groups,)),
+                dma((len(cuts),)),
                 dma,
                 dma((groups,)),
                 dma((nt - 1,)),
@@ -368,7 +391,7 @@
             in_specs=[vmem_spec] * 2,
             out_specs=(hbm_spec, hbm_spec),
             scratch_shapes=[dma((SPLIT + 1,))],
-        )(*held)
+        )(*(pltpu.with_memory_space_constraint(x, pltpu.VMEM) for x in held))
 
     placed = (
         P("seq", "tensor"),

time: 25.7 us -> 23.1 us (0.90)
  local copies, waits for them, and re-layouts: 1.5 us -> 0 us
  Pallas kernels: 23.4 us -> 22.3 us
    unnamed x4 -> x0, local copies, waits for them, and re-layouts: 1.5 us -> none
    pallas_call x1, Pallas kernels: 2.06 us -> 0.92 us  [shards(): pl.pallas_call(deliver, out_shape=(jax.ShapeDtypeStruct((tokens, width),...]
where the time goes in v4:
time: 23.1 us; the launch traced here: 22.9 us
  Pallas kernels  22.3 us (97%)
  between operations  0.64 us (3%)
    pallas_call x1, Pallas kernels, shards(): pl.pallas_call(functools.partial(kernel, n, nt, groups, cuts), out_shape=...  21.3 us
    pallas_call x1, Pallas kernels, shards(): pl.pallas_call(deliver, out_shape=(jax.ShapeDtypeStruct((tokens, width),...  0.92 us

profile of v4, /device:TPU:0, one launch (start us, length us, event | category | flops | bytes accessed | tf_op | source)
XLA Modules:
  0.0 22.9 jit_solution(4502440293029196883)
XLA Ops:
  0.6 21.3 %shard_map.77 = (bf16[512,768]{1,0:T(8,128)(2,1)S(1)}, bf16[16,768]{1,0:T(8,128)(2,1)S(1)}) custom-call(bf16[512,768]{1,0:T(8,128)(2,1)} %q_hbm.1, bf16[16,768]{1,0:T(8,128)(2,1)} %k_hbm.1, bf16[16,768]{1,0:T(8,128)(2,1)} %v_hbm.1, bf16[512,768]{1,0:T(8,128)(2,1)} %g_hbm.1, bf16[3072,768]{1,0:T(8,128)(2,1)} %kw_hbm.1, bf16[3072,768]{1,0:T(8,128)(2,1)} %vw_hbm.1), custom_call_target="tpu_custom_call" | custom-call | flops 1000000000 | bytes 12000000 | tf_op jit(solution)/shard_map/pallas_call | solution.py:341
  22.0 0.9 %shard_map.78 = (bf16[512,768]{1,0:T(8,128)(2,1)}, bf16[16,768]{1,0:T(8,128)(2,1)}) custom-call(bf16[512,768]{1,0:T(8,128)(2,1)S(1)} %get-tuple-element.4.gq_ref, bf16[16,768]{1,0:T(8,128)(2,1)S(1)} %get-tuple-element.5.rows_ref), custom_call_target="tpu_custom_call" | custom-call | tf_op jit(solution)/shard_map/pallas_call | solution.py:385

commit v5 on v4

--- a/solution.py
+++ b/solution.py
@@ -79,6 +79,7 @@
     parts,
     got,
     sums,
+    rest,
     out_send,
     out_got,
     head_acc,
@@ -243,12 +244,13 @@
     for copy in w_copies:
         copy.wait()
     rs_copies = []
-    for g in range(groups):
-        if g == 0:
-            query_grads(g)
-        cols = pl.ds(g * gw, gw)
-        arrived = got.at[:, :, cols]
-        pltpu.make_async_copy(arrived, arrived, aa_recv.at[g]).wait()
+    query_grads(0)
+    steps = [(0, groups - 1), (groups - 1, groups)] if groups > 1 else [(0, 1)]
+    for lo, hi in steps:
+        cols = pl.ds(lo * gw, (hi - lo) * gw)
+        for g in range(lo, hi):
+            arrived = got.at[:, :, pl.ds(g * gw, gw)]
+            pltpu.make_async_copy(arrived, arrived, aa_recv.at[g]).wait()
         sides = []
         for side in range(2):
             total = parts[side, my_rows, cols].astype(F32)
@@ -269,14 +271,18 @@
         for j in range(1, nt + 1):
             to = lax.rem(mt + j, nt)
             wr = pl.ds(pl.multiple_of(to * out_cols, out_cols), out_cols)
-            both = dot_nt(sides[0], w_buf[0, wr, cols]) + dot_nt(sides[1], w_buf[1, wr, cols])
-            new = both[:own] + both[own:]
-            if g:
+            new = dot_nt(w_buf[0, wr, cols], sides[0]) + dot_nt(w_buf[1, wr, cols], sides[1])
+            if lo:
                 new = new + sums[j - 1]
-            if g < groups - 1 or j == nt:
+            if hi < groups:
                 sums[j - 1] = new
+                continue
+            both = new.T
+            block = both[:own] + both[own:]
+            if j == nt:
+                rest[...] = block
             else:
-                out_send[j - 1] = new.astype(BF16)
+                out_send[j - 1] = block.astype(BF16)
                 copy = pltpu.make_async_remote_copy(
                     src_ref=out_send.at[j - 1],
                     dst_ref=out_got.at[j - 1],
@@ -293,7 +299,7 @@
     sent = kv_buf.at[:, others]
     pltpu.make_async_copy(sent, sent, ag_send).wait()
     pltpu.make_async_copy(got, got, aa_send).wait()
-    total = sums[nt - 1]
+    total = rest[...]
     for j, copy in enumerate(rs_copies):
         copy.wait_recv()
         total += out_got[j].astype(F32)
@@ -354,7 +360,8 @@
                 pltpu.VMEM((2, n * own, width), BF16),
                 pltpu.VMEM((2, n * own, width), BF16),
                 pltpu.VMEM((2, (n - 1) * own, width), BF16),
-                pltpu.VMEM((nt, own, out_cols), F32),
+                pltpu.VMEM((nt, out_cols, 2 * own), F32),
+                pltpu.VMEM((own, out_cols), F32),
                 pltpu.VMEM((nt - 1, own, out_cols), BF16),
                 pltpu.VMEM((nt - 1, own, out_cols), BF16),
                 pltpu.VMEM((2, n * own, HD), F32),

time: 23.1 us -> 23.5 us (1.017)
  Pallas kernels: 22.3 us -> 22.7 us
    pallas_call x1, Pallas kernels: 21.3 us -> 21.7 us  [shards(): pl.pallas_call(functools.partial(kernel, n, nt, groups, cuts), out_shape=...]
where the time goes in v5:
time: 23.5 us; the launch traced here: 23.3 us
  Pallas kernels  22.7 us (97%)
  between operations  0.64 us (3%)
    pallas_call x1, Pallas kernels, shards(): pl.pallas_call(functools.partial(kernel, n, nt, groups, cuts), out_shape=...  21.7 us
    pallas_call x1, Pallas kernels, shards(): pl.pallas_call(deliver, out_shape=(jax.ShapeDtypeStruct((tokens, width),...  0.92 us

profile of v5, /device:TPU:0, one launch (start us, length us, event | category | flops | bytes accessed | tf_op | source)
XLA Modules:
  0.0 23.3 jit_solution(5294804358605290859)
XLA Ops:
  0.6 21.7 %shard_map.77 = (bf16[512,768]{1,0:T(8,128)(2,1)S(1)}, bf16[16,768]{1,0:T(8,128)(2,1)S(1)}) custom-call(bf16[512,768]{1,0:T(8,128)(2,1)} %q_hbm.1, bf16[16,768]{1,0:T(8,128)(2,1)} %k_hbm.1, bf16[16,768]{1,0:T(8,128)(2,1)} %v_hbm.1, bf16[512,768]{1,0:T(8,128)(2,1)} %g_hbm.1, bf16[3072,768]{1,0:T(8,128)(2,1)} %kw_hbm.1, bf16[3072,768]{1,0:T(8,128)(2,1)} %vw_hbm.1), custom_call_target="tpu_custom_call" | custom-call | flops 1000000000 | bytes 12000000 | tf_op jit(solution)/shard_map/pallas_call | solution.py:347
  22.4 0.9 %shard_map.78 = (bf16[512,768]{1,0:T(8,128)(2,1)}, bf16[16,768]{1,0:T(8,128)(2,1)}) custom-call(bf16[512,768]{1,0:T(8,128)(2,1)S(1)} %get-tuple-element.4.gq_ref, bf16[16,768]{1,0:T(8,128)(2,1)S(1)} %get-tuple-element.5.rows_ref), custom_call_target="tpu_custom_call" | custom-call | tf_op jit(solution)/shard_map/pallas_call | solution.py:392

commit v6 on v5

--- a/solution.py
+++ b/solution.py
@@ -77,6 +77,8 @@
     w_buf,
     kv_buf,
     parts,
+    mate_got,
+    pair_buf,
     got,
     sums,
     rest,
@@ -88,6 +90,10 @@
     w_sem,
     ag_send,
     ag_recv,
+    fw_send,
+    fw_recv,
+    sw_send,
+    sw_recv,
     aa_send,
     aa_recv,
     rs_send,
@@ -101,21 +107,31 @@
     per = heads // groups
     gw = per * HD
     out_cols = rows_ref.shape[1]
-    my_rows = pl.ds(pl.multiple_of(me * own, own), own)
+    pairs = n // 2
+    half = pairs * own
+    parity = lax.rem(me, 2)
+    mine = me // 2
+    mate = me + 1 - 2 * parity
+    my_at = pl.multiple_of(parity * half, half)
+    mate_at = pl.multiple_of((1 - parity) * half, half)
+    pair_rows = pl.ds(pl.multiple_of(mine * own, own), own)
+    my_rows = pl.ds(pl.multiple_of(my_at + mine * own, own), own)
 
     barrier = pltpu.get_barrier_semaphore()
 
+    def peer(k):
+        return 2 * lax.rem(mine + k, pairs) + parity
+
     def greet_seq(k):
-        pl.semaphore_signal(
-            barrier, inc=1, device_id={"seq": lax.rem(me + k, n)}, device_id_type=MESH
-        )
+        pl.semaphore_signal(barrier, inc=1, device_id={"seq": peer(k)}, device_id_type=MESH)
 
     def greet_tensor(k):
         pl.semaphore_signal(
             barrier, inc=1, device_id={"tensor": lax.rem(mt + k, nt)}, device_id_type=MESH
         )
 
-    each(1, n, greet_seq)
+    each(1, pairs, greet_seq)
+    pl.semaphore_signal(barrier, inc=1, device_id={"seq": mate}, device_id_type=MESH)
     each(1, nt, greet_tensor)
     own_copies = [
         pltpu.make_async_copy(k_hbm, kv_buf.at[0, my_rows], own_sem.at[0]),
@@ -132,7 +148,7 @@
 
     for copy in own_copies:
         copy.wait()
-    pl.semaphore_wait(barrier, n + nt - 2)
+    pl.semaphore_wait(barrier, pairs + nt - 1)
 
     for c, (first, count) in enumerate(cuts):
         cols = pl.ds(first * HD, count * HD)
@@ -144,11 +160,11 @@
                 dst_ref=block,
                 send_sem=ag_send,
                 recv_sem=ag_recv.at[c],
-                device_id={"seq": lax.rem(me + k, n)},
+                device_id={"seq": peer(k)},
                 device_id_type=MESH,
             ).start()
 
-        each(1, n, send_rows)
+        each(1, pairs, send_rows)
 
     w_copies = [
         pltpu.make_async_copy(kw_hbm, w_buf.at[0], w_sem.at[0]),
@@ -160,14 +176,58 @@
         copy.wait()
 
     ref_rows = n * own
-    others = pl.ds(0, (n - 1) * own)
+    others = pl.ds(0, half - own)
     small = ref_rows <= 256
 
+    def to_mate(src, dst, send_sem, recv_sem):
+        return pltpu.make_async_remote_copy(
+            src_ref=src,
+            dst_ref=dst,
+            send_sem=send_sem,
+            recv_sem=recv_sem,
+            device_id={"seq": mate},
+            device_id_type=MESH,
+        )
+
+    def forward_rows(c):
+        first, count = cuts[c]
+        cols = pl.ds(first * HD, count * HD)
+        arrived = kv_buf.at[:, others, cols]
+        pltpu.make_async_copy(arrived, arrived, ag_recv.at[c]).wait()
+        block = kv_buf.at[:, pl.ds(my_at, half), cols]
+        copy = to_mate(block, block, fw_send.at[c], fw_recv.at[c])
+        copy.start()
+        forwards.append(copy)
+
     def await_rows(c):
-        first, count = cuts[c]
-        arrived = kv_buf.at[:, others, pl.ds(first * HD, count * HD)]
-        pltpu.make_async_copy(arrived, arrived, ag_recv.at[c]).wait()
-
+        if c + 1 < len(cuts):
+            forward_rows(c + 1)
+        forwards[c].wait_recv()
+
+    def send_pair_sums(g):
+        cols = pl.ds(g * gw, gw)
+        swaps[g].wait_recv()
+        for side in range(2):
+            both = parts[side, pl.ds(my_at, half), cols].astype(F32)
+            both += mate_got[side, :, cols].astype(F32)
+            pair_buf[side, :, cols] = both.astype(BF16)
+
+        def send_one(k):
+            to = lax.rem(mine + k, pairs)
+            pltpu.make_async_remote_copy(
+                src_ref=pair_buf.at[:, pl.ds(pl.multiple_of(to * own, own), own), cols],
+                dst_ref=got.at[:, pl.ds((k - 1) * own, own), cols],
+                send_sem=aa_send,
+                recv_sem=aa_recv.at[g],
+                device_id={"seq": 2 * to + parity},
+                device_id_type=MESH,
+            ).start()
+
+        each(1, pairs, send_one)
+
+    forwards = []
+    swaps = []
+    forward_rows(0)
     starts = [first for first, _ in cuts]
     for g in range(groups):
         cols = pl.ds(g * gw, gw)
@@ -214,18 +274,16 @@
                     await_rows(starts.index(head))
             lax.fori_loop(g * per, (g + 1) * per, lambda h, c: (one_head(h), c)[1], 0)
 
-        def send_parts(k, g=g, cols=cols):
-            to = lax.rem(me + k, n)
-            pltpu.make_async_remote_copy(
-                src_ref=parts.at[:, pl.ds(pl.multiple_of(to * own, own), own), cols],
-                dst_ref=got.at[:, pl.ds((k - 1) * own, own), cols],
-                send_sem=aa_send,
-                recv_sem=aa_recv.at[g],
-                device_id={"seq": to},
-                device_id_type=MESH,
-            ).start()
-
-        each(1, n, send_parts)
+        swap = to_mate(
+            parts.at[:, pl.ds(mate_at, half), cols],
+            mate_got.at[:, :, cols],
+            sw_send.at[g],
+            sw_recv.at[g],
+        )
+        swap.start()
+        swaps.append(swap)
+        if g:
+            send_pair_sums(g - 1)
 
     def query_grads(g):
         def one_head(head):
@@ -241,10 +299,11 @@
         else:
             lax.fori_loop(g * per, (g + 1) * per, lambda h, c: (one_head(h), c)[1], 0)
 
+    rs_copies = []
+    query_grads(0)
+    send_pair_sums(groups - 1)
     for copy in w_copies:
         copy.wait()
-    rs_copies = []
-    query_grads(0)
     steps = [(0, groups - 1), (groups - 1, groups)] if groups > 1 else [(0, 1)]
     for lo, hi in steps:
         cols = pl.ds(lo * gw, (hi - lo) * gw)
@@ -254,13 +313,14 @@
         sides = []
         for side in range(2):
             total = parts[side, my_rows, cols].astype(F32)
+            total += mate_got[side, pair_rows, cols].astype(F32)
             if n <= 8:
-                for k in range(n - 1):
+                for k in range(pairs - 1):
                     total += got[side, k * own : (k + 1) * own, cols].astype(F32)
             else:
                 total = lax.fori_loop(
                     0,
-                    n - 1,
+                    pairs - 1,
                     lambda k, acc: acc
                     + got[side, pl.ds(pl.multiple_of(k * own, own), own), cols].astype(F32),
                     total,
@@ -271,14 +331,13 @@
         for j in range(1, nt + 1):
             to = lax.rem(mt + j, nt)
             wr = pl.ds(pl.multiple_of(to * out_cols, out_cols), out_cols)
-            new = dot_nt(w_buf[0, wr, cols], sides[0]) + dot_nt(w_buf[1, wr, cols], sides[1])
+            both = dot_nt(sides[0], w_buf[0, wr, cols]) + dot_nt(sides[1], w_buf[1, wr, cols])
+            block = both[:own] + both[own:]
             if lo:
-                new = new + sums[j - 1]
+                block = block + sums[j - 1]
             if hi < groups:
-                sums[j - 1] = new
+                sums[j - 1] = block
                 continue
-            both = new.T
-            block = both[:own] + both[own:]
             if j == nt:
                 rest[...] = block
             else:
@@ -299,6 +358,8 @@
     sent = kv_buf.at[:, others]
     pltpu.make_async_copy(sent, sent, ag_send).wait()
     pltpu.make_async_copy(got, got, aa_send).wait()
+    for copy in forwards + swaps:
+        copy.wait_send()
     total = rest[...]
     for j, copy in enumerate(rs_copies):
         copy.wait_recv()
@@ -306,16 +367,6 @@
     rows_ref[...] = total.astype(BF16)
     for copy in rs_copies:
         copy.wait_send()
-
-
-def gather_cuts(heads):
-    cuts = []
-    at = 0
-    while at < heads:
-        count = min(1 if at < 2 else 2, heads - at)
-        cuts.append((at, count))
-        at += count
-    return cuts
 
 
 def deliver(gq_ref, rows_ref, gq_out, rows_out, sem):
@@ -339,7 +390,8 @@
         features = key_weight.shape[0]
         heads = width // HD
         groups = 3 if heads % 3 == 0 else 1
-        cuts = gather_cuts(heads)
+        per = heads // groups
+        cuts = [(g * per, per) for g in range(groups)]
         out_cols = features // nt
         hbm_spec = pl.BlockSpec(memory_space=pltpu.HBM)
         vmem_spec = pl.BlockSpec(memory_space=pltpu.VMEM)
@@ -359,8 +411,10 @@
                 pltpu.VMEM((2, features, width), BF16),
                 pltpu.VMEM((2, n * own, width), BF16),
                 pltpu.VMEM((2, n * own, width), BF16),
-                pltpu.VMEM((2, (n - 1) * own, width), BF16),
-                pltpu.VMEM((nt, out_cols, 2 * own), F32),
+                pltpu.VMEM((2, n // 2 * own, width), BF16),
+                pltpu.VMEM((2, n // 2 * own, width), BF16),
+                pltpu.VMEM((2, (n // 2 - 1) * own, width), BF16),
+                pltpu.VMEM((nt, own, out_cols), F32),
                 pltpu.VMEM((own, out_cols), F32),
                 pltpu.VMEM((nt - 1, own, out_cols), BF16),
                 pltpu.VMEM((nt - 1, own, out_cols), BF16),
@@ -370,6 +424,10 @@
                 dma((2,)),
                 dma,
                 dma((len(cuts),)),
+                dma((len(cuts),)),
+                dma((len(cuts),)),
+                dma((groups,)),
+                dma((groups,)),
                 dma,
                 dma((groups,)),
                 dma((nt - 1,)),

time: 23.5 us -> 24 us (1.021)
  Pallas kernels: 22.7 us -> 23.2 us
    pallas_call x1, Pallas kernels: 21.7 us -> 22.3 us  [shards(): pl.pallas_call(functools.partial(kernel, n, nt, groups, cuts), out_shape=...]
where the time goes in v6:
time: 24 us; the launch traced here: 23.8 us
  Pallas kernels  23.2 us (97%)
  between operations  0.64 us (3%)
    pallas_call x1, Pallas kernels, shards(): pl.pallas_call(functools.partial(kernel, n, nt, groups, cuts), out_shape=...  22.3 us
    pallas_call x1, Pallas kernels, shards(): pl.pallas_call(deliver, out_shape=(jax.ShapeDtypeStruct((tokens, width),...  0.92 us

profile of v6, /device:TPU:0, one launch (start us, length us, event | category | flops | bytes accessed | tf_op | source)
XLA Modules:
  0.0 23.8 jit_solution(3582736473235667357)
XLA Ops:
  0.6 22.3 %shard_map.77 = (bf16[512,768]{1,0:T(8,128)(2,1)S(1)}, bf16[16,768]{1,0:T(8,128)(2,1)S(1)}) custom-call(bf16[512,768]{1,0:T(8,128)(2,1)} %q_hbm.1, bf16[16,768]{1,0:T(8,128)(2,1)} %k_hbm.1, bf16[16,768]{1,0:T(8,128)(2,1)} %v_hbm.1, bf16[512,768]{1,0:T(8,128)(2,1)} %g_hbm.1, bf16[3072,768]{1,0:T(8,128)(2,1)} %kw_hbm.1, bf16[3072,768]{1,0:T(8,128)(2,1)} %vw_hbm.1), custom_call_target="tpu_custom_call" | custom-call | flops 1000000000 | bytes 12000000 | tf_op jit(solution)/shard_map/pallas_call | solution.py:399
  22.9 0.9 %shard_map.78 = (bf16[512,768]{1,0:T(8,128)(2,1)}, bf16[16,768]{1,0:T(8,128)(2,1)}) custom-call(bf16[512,768]{1,0:T(8,128)(2,1)S(1)} %get-tuple-element.4.gq_ref, bf16[16,768]{1,0:T(8,128)(2,1)S(1)} %get-tuple-element.5.rows_ref), custom_call_target="tpu_custom_call" | custom-call | tf_op jit(solution)/shard_map/pallas_call | solution.py:450

commit v7 on v4

--- a/solution.py
+++ b/solution.py
@@ -44,18 +44,23 @@
     return jnp.dot(a, b, preferred_element_type=F32)
 
 
-def attend(query, key, value, grad):
-    scores = dot_nt(key, query)
-    grad_probs = dot_nt(value, grad)
+def score(query, key, value, grad):
+    return dot_nt(key, query), dot_nt(value, grad)
+
+
+def soften(scores, grad_probs):
     top = jnp.max(scores, axis=0, keepdims=True)
     weights = jnp.exp2((scores - top) * EXP_SCALE)
     inverse = 1.0 / jnp.sum(weights, axis=0, keepdims=True)
     probs = weights * inverse
     delta = jnp.sum(probs * grad_probs, axis=0, keepdims=True)
     grad_scores = (probs * (grad_probs - delta)).astype(BF16)
-    grad_key = dot_nn(grad_scores, query)
-    grad_value = dot_nn(probs.astype(BF16), grad)
-    return grad_scores, grad_key, grad_value
+    return grad_scores, probs.astype(BF16)
+
+
+def attend(query, key, value, grad):
+    grad_scores, probs = soften(*score(query, key, value, grad))
+    return grad_scores, dot_nn(grad_scores, query), dot_nn(probs, grad)
 
 
 def kernel(
@@ -149,10 +154,13 @@
 
         each(1, n, send_rows)
 
-    w_copies = [
-        pltpu.make_async_copy(kw_hbm, w_buf.at[0], w_sem.at[0]),
-        pltpu.make_async_copy(vw_hbm, w_buf.at[1], w_sem.at[1]),
-    ]
+    w_copies = []
+    for b in range(nt):
+        wr = pl.ds(b * out_cols, out_cols)
+        for side, ref in enumerate((kw_hbm, vw_hbm)):
+            w_copies.append(
+                pltpu.make_async_copy(ref.at[wr], w_buf.at[side, wr], w_sem.at[side, b])
+            )
     for copy in w_copies:
         copy.start()
     for copy in in_copies:
@@ -178,35 +186,53 @@
                 hc = pl.ds(pl.multiple_of(head * HD, HD), HD)
             key = kv_buf[0, :, hc]
             value = kv_buf[1, :, hc]
-            if small:
-                grad_key = grad_value = None
-                for lo in range(0, tokens, CHUNK):
-                    tok = slice(lo, min(lo + CHUNK, tokens))
-                    ds, gk, gv = attend(q_buf[tok, hc], key, value, g_buf[tok, hc])
-                    ds_buf[head, :, tok] = ds
-                    grad_key = gk if grad_key is None else grad_key + gk
-                    grad_value = gv if grad_value is None else grad_value + gv
-            else:
-                head_acc[...] = jnp.zeros_like(head_acc)
-
-                def chunk(c, carry):
-                    tok = pl.ds(pl.multiple_of(c * HD, HD), HD)
-                    ds, gk, gv = attend(q_buf[tok, hc], key, value, g_buf[tok, hc])
-                    ds_buf[head, :, tok] = ds
-                    head_acc[0] += gk
-                    head_acc[1] += gv
-                    return carry
-
-                lax.fori_loop(0, tokens // HD, chunk, 0)
-                grad_key, grad_value = head_acc[0], head_acc[1]
+            head_acc[...] = jnp.zeros_like(head_acc)
+
+            def chunk(c, carry):
+                tok = pl.ds(pl.multiple_of(c * HD, HD), HD)
+                ds, gk, gv = attend(q_buf[tok, hc], key, value, g_buf[tok, hc])
+                ds_buf[head, :, tok] = ds
+                head_acc[0] += gk
+                head_acc[1] += gv
+                return carry
+
+            lax.fori_loop(0, tokens // HD, chunk, 0)
+            grad_key, grad_value = head_acc[0], head_acc[1]
             parts[0, :, hc] = (grad_key * SCALE).astype(BF16)
             parts[1, :, hc] = grad_value.astype(BF16)
 
         if small:
-            for head in range(g * per, (g + 1) * per):
-                if head in starts:
-                    await_rows(starts.index(head))
-                one_head(head)
+            units = [
+                (head, slice(lo, min(lo + CHUNK, tokens)))
+                for head in range(g * per, (g + 1) * per)
+                for lo in range(0, tokens, CHUNK)
+            ]
+            scored, soft, totals = {}, {}, {}
+            for u in range(-1, len(units) + 1):
+                if u + 1 < len(units):
+                    head, tok = units[u + 1]
+                    if tok.start == 0 and head in starts:
+                        await_rows(starts.index(head))
+                    hc = slice(head * HD, (head + 1) * HD)
+                    scored[u + 1] = score(
+                        q_buf[tok, hc], kv_buf[0, :, hc], kv_buf[1, :, hc], g_buf[tok, hc]
+                    )
+                if 0 <= u - 1:
+                    head, tok = units[u - 1]
+                    hc = slice(head * HD, (head + 1) * HD)
+                    ds, probs = soft.pop(u - 1)
+                    gk, gv = dot_nn(ds, q_buf[tok, hc]), dot_nn(probs, g_buf[tok, hc])
+                    if head in totals:
+                        gk, gv = totals[head][0] + gk, totals[head][1] + gv
+                    totals[head] = (gk, gv)
+                    if tok.stop == tokens:
+                        parts[0, :, hc] = (gk * SCALE).astype(BF16)
+                        parts[1, :, hc] = gv.astype(BF16)
+                if 0 <= u < len(units):
+                    head, tok = units[u]
+                    ds, probs = soften(*scored.pop(u))
+                    ds_buf[head, :, tok] = ds
+                    soft[u] = (ds, probs)
         else:
             for head in range(g * per, (g + 1) * per):
                 if head in starts:
@@ -360,7 +386,7 @@
                 pltpu.VMEM((2, n * own, HD), F32),
                 dma((2,)),
                 dma((2,)),
-                dma((2,)),
+                dma((2, nt)),
                 dma,
                 dma((len(cuts),)),
                 dma,

time: 23.1 us -> 22.9 us (level)
  no operation moved by 1% of the time
where the time goes in v7:
time: 22.9 us; the launch traced here: 22.7 us
  Pallas kernels  22.1 us (97%)
  between operations  0.64 us (3%)
    pallas_call x1, Pallas kernels, shards(): pl.pallas_call(functools.partial(kernel, n, nt, groups, cuts), out_shape=...  21.2 us
    pallas_call x1, Pallas kernels, shards(): pl.pallas_call(deliver, out_shape=(jax.ShapeDtypeStruct((tokens, width),...  0.92 us

profile of v7, /device:TPU:0, one launch (start us, length us, event | category | flops | bytes accessed | tf_op | source)
XLA Modules:
  0.0 22.7 jit_solution(12090748313255217738)
XLA Ops:
  0.6 21.2 %shard_map.77 = (bf16[512,768]{1,0:T(8,128)(2,1)S(1)}, bf16[16,768]{1,0:T(8,128)(2,1)S(1)}) custom-call(bf16[512,768]{1,0:T(8,128)(2,1)} %q_hbm.1, bf16[16,768]{1,0:T(8,128)(2,1)} %k_hbm.1, bf16[16,768]{1,0:T(8,128)(2,1)} %v_hbm.1, bf16[512,768]{1,0:T(8,128)(2,1)} %g_hbm.1, bf16[3072,768]{1,0:T(8,128)(2,1)} %kw_hbm.1, bf16[3072,768]{1,0:T(8,128)(2,1)} %vw_hbm.1), custom_call_target="tpu_custom_call" | custom-call | flops 1000000000 | bytes 12000000 | tf_op jit(solution)/shard_map/pallas_call | solution.py:367
  21.8 0.9 %shard_map.78 = (bf16[512,768]{1,0:T(8,128)(2,1)}, bf16[16,768]{1,0:T(8,128)(2,1)}) custom-call(bf16[512,768]{1,0:T(8,128)(2,1)S(1)} %get-tuple-element.4.gq_ref, bf16[16,768]{1,0:T(8,128)(2,1)S(1)} %get-tuple-element.5.rows_ref), custom_call_target="tpu_custom_call" | custom-call | tf_op jit(solution)/shard_map/pallas_call | solution.py:411

commit v8 on v7

--- a/solution.py
+++ b/solution.py
@@ -134,6 +134,15 @@
     for copy in in_copies:
         copy.start()
 
+    w_copies = []
+    for b in range(nt):
+        wr = pl.ds(b * out_cols, out_cols)
+        for side, ref in enumerate((kw_hbm, vw_hbm)):
+            w_copies.append(
+                pltpu.make_async_copy(ref.at[wr], w_buf.at[side, wr], w_sem.at[side, b])
+            )
+    for copy in w_copies:
+        copy.start()
     for copy in own_copies:
         copy.wait()
     pl.semaphore_wait(barrier, n + nt - 2)
@@ -154,15 +163,6 @@
 
         each(1, n, send_rows)
 
-    w_copies = []
-    for b in range(nt):
-        wr = pl.ds(b * out_cols, out_cols)
-        for side, ref in enumerate((kw_hbm, vw_hbm)):
-            w_copies.append(
-                pltpu.make_async_copy(ref.at[wr], w_buf.at[side, wr], w_sem.at[side, b])
-            )
-    for copy in w_copies:
-        copy.start()
     for copy in in_copies:
         copy.wait()
 
@@ -270,7 +270,7 @@
         copy.wait()
     rs_copies = []
     for g in range(groups):
-        if g == 0:
+        if g < groups - 1:
             query_grads(g)
         cols = pl.ds(g * gw, gw)
         arrived = got.at[:, :, cols]
@@ -314,8 +314,7 @@
                 copy.start()
                 rs_copies.append(copy)
 
-    for g in range(1, groups):
-        query_grads(g)
+    query_grads(groups - 1)
     sent = kv_buf.at[:, others]
     pltpu.make_async_copy(sent, sent, ag_send).wait()
     pltpu.make_async_copy(got, got, aa_send).wait()
@@ -332,7 +331,7 @@
     cuts = []
     at = 0
     while at < heads:
-        count = min(1 if at < 2 else 2, heads - at)
+        count = min(2, heads - at)
         cuts.append((at, count))
         at += count
     return cuts

time: 22.9 us -> 24.7 us (1.079)
  Pallas kernels: 22.1 us -> 23.9 us
    pallas_call x1, Pallas kernels: 21.2 us -> 23 us  [shards(): pl.pallas_call(functools.partial(kernel, n, nt, groups, cuts), out_shape=...]
where the time goes in v8:
time: 24.7 us; the launch traced here: 24.5 us
  Pallas kernels  23.9 us (97%)
  between operations  0.64 us (3%)
    pallas_call x1, Pallas kernels, shards(): pl.pallas_call(functools.partial(kernel, n, nt, groups, cuts), out_shape=...  23 us
    pallas_call x1, Pallas kernels, shards(): pl.pallas_call(deliver, out_shape=(jax.ShapeDtypeStruct((tokens, width),...  0.92 us

profile of v8, /device:TPU:0, one launch (start us, length us, event | category | flops | bytes accessed | tf_op | source)
XLA Modules:
  0.0 24.5 jit_solution(4739975060071677114)
XLA Ops:
  0.6 23.0 %shard_map.77 = (bf16[512,768]{1,0:T(8,128)(2,1)S(1)}, bf16[16,768]{1,0:T(8,128)(2,1)S(1)}) custom-call(bf16[512,768]{1,0:T(8,128)(2,1)} %q_hbm.1, bf16[16,768]{1,0:T(8,128)(2,1)} %k_hbm.1, bf16[16,768]{1,0:T(8,128)(2,1)} %v_hbm.1, bf16[512,768]{1,0:T(8,128)(2,1)} %g_hbm.1, bf16[3072,768]{1,0:T(8,128)(2,1)} %kw_hbm.1, bf16[3072,768]{1,0:T(8,128)(2,1)} %vw_hbm.1), custom_call_target="tpu_custom_call" | custom-call | flops 1000000000 | bytes 12000000 | tf_op jit(solution)/shard_map/pallas_call | solution.py:366
  23.6 0.9 %shard_map.78 = (bf16[512,768]{1,0:T(8,128)(2,1)}, bf16[16,768]{1,0:T(8,128)(2,1)}) custom-call(bf16[512,768]{1,0:T(8,128)(2,1)S(1)} %get-tuple-element.4.gq_ref, bf16[16,768]{1,0:T(8,128)(2,1)S(1)} %get-tuple-element.5.rows_ref), custom_call_target="tpu_custom_call" | custom-call | tf_op jit(solution)/shard_map/pallas_call | solution.py:410

commit v9 on v7

--- a/solution.py
+++ b/solution.py
@@ -161,7 +161,8 @@
             w_copies.append(
                 pltpu.make_async_copy(ref.at[wr], w_buf.at[side, wr], w_sem.at[side, b])
             )
-    for copy in w_copies:
+    lot = -(-len(w_copies) // groups)
+    for copy in w_copies[:lot]:
         copy.start()
     for copy in in_copies:
         copy.wait()
@@ -251,6 +252,8 @@
             ).start()
 
         each(1, n, send_parts)
+        for copy in w_copies[(g + 1) * lot : (g + 2) * lot]:
+            copy.start()
 
     def query_grads(g):
         def one_head(head):

time: 22.9 us -> 22.9 us (level)
  no operation moved by 1% of the time
where the time goes in v9:
time: 22.9 us; the launch traced here: 22.7 us
  Pallas kernels  22.1 us (97%)
  between operations  0.64 us (3%)
    pallas_call x1, Pallas kernels, shards(): pl.pallas_call(functools.partial(kernel, n, nt, groups, cuts), out_shape=...  21.2 us
    pallas_call x1, Pallas kernels, shards(): pl.pallas_call(deliver, out_shape=(jax.ShapeDtypeStruct((tokens, width),...  0.92 us

profile of v9, /device:TPU:0, one launch (start us, length us, event | category | flops | bytes accessed | tf_op | source)
XLA Modules:
  0.0 22.7 jit_solution(16782007665731588913)
XLA Ops:
  0.6 21.2 %shard_map.77 = (bf16[512,768]{1,0:T(8,128)(2,1)S(1)}, bf16[16,768]{1,0:T(8,128)(2,1)S(1)}) custom-call(bf16[512,768]{1,0:T(8,128)(2,1)} %q_hbm.1, bf16[16,768]{1,0:T(8,128)(2,1)} %k_hbm.1, bf16[16,768]{1,0:T(8,128)(2,1)} %v_hbm.1, bf16[512,768]{1,0:T(8,128)(2,1)} %g_hbm.1, bf16[3072,768]{1,0:T(8,128)(2,1)} %kw_hbm.1, bf16[3072,768]{1,0:T(8,128)(2,1)} %vw_hbm.1), custom_call_target="tpu_custom_call" | custom-call | flops 1000000000 | bytes 12000000 | tf_op jit(solution)/shard_map/pallas_call | solution.py:370
  21.8 0.9 %shard_map.78 = (bf16[512,768]{1,0:T(8,128)(2,1)}, bf16[16,768]{1,0:T(8,128)(2,1)}) custom-call(bf16[512,768]{1,0:T(8,128)(2,1)S(1)} %get-tuple-element.4.gq_ref, bf16[16,768]{1,0:T(8,128)(2,1)S(1)} %get-tuple-element.5.rows_ref), custom_call_target="tpu_custom_call" | custom-call | tf_op jit(solution)/shard_map/pallas_call | solution.py:414
